TPU v7x, 32 devices: a whole 2x2x4 slice. The times are simulated.
32 devices in a mesh: groups: 2 (over x), tile: 4 (over y, core), led: 4 (over z).
Axes of the slice: x: 2, y: 2, z: 4, core: 2. Of those that a mesh axis runs over, the one named last changes fastest.
Arguments:
- spectra: bfloat16 [16, 2, 384, 384], P(('groups', 'tile')), parts along dimension 0, may hold values from -6 to 6
- pupils: float32 [16, 2, 256, 256], P(('groups', 'tile')), parts along dimension 0, may hold values from -3 to 3
- amplitudes: bfloat16 [16, 8, 256, 256], P(('groups', 'tile'), 'led'), parts along dimension 0, may hold values from 0.19921875 to 2
- offsets: int32 [16, 8, 2], P(('groups', 'tile'), 'led'), parts along dimension 0, may hold values from 0 to 128
- positions: int32 [16, 2], P(('groups', 'tile')), parts along dimension 0, may hold values from 0 to 2047
Outputs:
- refitted: float32 [16, 2, 256, 256], P(('groups', 'tile'), None, 'led'), parts along dimension 0
There are 2 independent parts, one for each index of `groups`. A program takes and returns all parts, laid end to end along the dimension named above; each array names one. Nothing has to cross between parts.
Inputs may be any that keep to these rules, and one draw needn't show every extreme that they name: `offsets`: every sub-spectrum lies inside its tile's spectrum.
All inputs are finite; a program needn't handle non-finite values.
Results may differ from a plain program's by a relative error of at most 0.0022.
Values sent between devices are 32-bit elements; how exact they have to be, the bound alone decides.
A program may use at most 64 MiB of HBM per device.

v0:
```python
import math

import jax
import jax.numpy as jnp
from jax import lax
from jax.sharding import PartitionSpec as P

DEG = 5
FIELD = 2048


RIDGE = 0.05
FLOOR = 0.25


def fourier_tables(length, sign):
    index = jnp.arange(length, dtype=jnp.int32)
    product = index[:, None] * index[None, :] % length
    angle = product.astype(jnp.float32) * (2.0 * math.pi / length)
    factor = 1.0 / math.sqrt(length)
    return (
        (jnp.cos(angle) * factor).astype(jnp.bfloat16),
        (sign * jnp.sin(angle) * factor).astype(jnp.bfloat16),
    )


def fourier_square(real_part, imag_part, table_re, table_im):
    length = real_part.shape[0]
    left_side = jnp.concatenate([table_re, table_im], 0)
    right_side = jnp.concatenate([real_part, imag_part], 1)
    first_prod = jnp.dot(left_side, right_side, preferred_element_type=jnp.float32)
    middle_re = (first_prod[:length, :length] - first_prod[length:, length:]).astype(jnp.bfloat16)
    middle_im = (first_prod[:length, length:] + first_prod[length:, :length]).astype(jnp.bfloat16)
    left_side = jnp.concatenate([middle_re, middle_im], 0)
    right_side = jnp.concatenate([table_re, table_im], 1)
    second_prod = jnp.dot(left_side, right_side, preferred_element_type=jnp.float32)
    result_re = second_prod[:length, :length] - second_prod[length:, length:]
    result_im = second_prod[:length, length:] + second_prod[length:, :length]
    return (result_re, result_im)


def led_update(spectrum, pupil_tile, amplitude, offset, tables):
    length = pupil_tile.shape[1]
    zero_index = jnp.zeros((), jnp.int32)
    window = lax.dynamic_slice(
        spectrum, (zero_index, offset[0], offset[1]), (2, length, length)
    ).astype(jnp.float32)
    window_re, window_im = (window[0], window[1])
    field_re = (pupil_tile[0] * window_re - pupil_tile[1] * window_im).astype(jnp.bfloat16)
    field_im = (pupil_tile[0] * window_im + pupil_tile[1] * window_re).astype(jnp.bfloat16)
    wave_re, wave_im = fourier_square(field_re, field_im, tables[2], tables[3])
    magnitude = jnp.sqrt(wave_re * wave_re + wave_im * wave_im)
    amp_ratio = amplitude.astype(jnp.float32) / jnp.maximum(magnitude, FLOOR) - 1.0
    diff_re = (wave_re * amp_ratio).astype(jnp.bfloat16)
    diff_im = (wave_im * amp_ratio).astype(jnp.bfloat16)
    delta_re, delta_im = fourier_square(diff_re, diff_im, tables[0], tables[1])
    grad_re = window_re * delta_re + window_im * delta_im
    grad_im = window_re * delta_im - window_im * delta_re
    peak_value = jnp.max(window_re * window_re + window_im * window_im)
    return (jnp.stack([grad_re, grad_im]), peak_value)


def tile_pass(spectrum, pupil_tile, amplitude_set, offset_set, tables):

    def advance(carry, items):
        term, peak_value = led_update(spectrum, pupil_tile, items[0], items[1], tables)
        return ((carry[0] + term, carry[1] + peak_value), None)

    start_state = (jnp.zeros(pupil_tile.shape, jnp.float32), jnp.zeros((), jnp.float32))
    final_state, unused = lax.scan(advance, start_state, (amplitude_set, offset_set))
    return final_state


def legendre_basis(positions):
    coords = positions.astype(jnp.float32) * (2.0 / (FIELD - 1)) - 1.0

    def series(values):
        polys = [jnp.ones_like(values), values]
        for degree in range(2, DEG + 1):
            polys.append(
                ((2 * degree - 1) * values * polys[-1] - (degree - 1) * polys[-2]) / degree
            )
        return polys

    along_x = series(coords[:, 0])
    along_y = series(coords[:, 1])
    columns = [
        along_x[first] * along_y[order_sum - first]
        for order_sum in range(DEG + 1)
        for first in range(order_sum + 1)
    ]
    return jnp.stack(columns, 1)


def per_device(spectra, pupils, amplitudes, offsets, positions):
    length = pupils.shape[2]
    forward_re, forward_im = fourier_tables(length, -1.0)
    inverse_re, inverse_im = fourier_tables(length, 1.0)
    tables = (forward_re, forward_im, inverse_re, inverse_im)
    gradient, peak_sums = lax.map(
        lambda items: tile_pass(items[0], items[1], items[2], items[3], tables),
        (spectra, pupils, amplitudes, offsets),
    )
    led_count = amplitudes.shape[1] * lax.axis_size("led")
    row_count = length // lax.axis_size("led")
    row_start = lax.axis_index("led") * row_count
    grad_total, peak_total = lax.psum((gradient, peak_sums), "led")
    grad_rows = lax.dynamic_slice_in_dim(grad_total, row_start, row_count, 2)
    own_rows = lax.dynamic_slice_in_dim(pupils, row_start, row_count, 2)
    updated = own_rows + grad_rows / (peak_total / led_count)[:, None, None, None]
    basis_rows = legendre_basis(positions)
    term_count = basis_rows.shape[1]
    tile_count = basis_rows.shape[0] * lax.axis_size("tile")
    piece_rows = lax.all_gather(updated, "tile", axis=0, tiled=True)
    piece_basis = lax.all_gather(basis_rows, "tile", axis=0, tiled=True)
    next_proj = jnp.einsum(
        "tk,tcuv->kcuv", piece_basis, piece_rows, precision=lax.Precision.HIGHEST
    )
    next_gram = jnp.dot(
        piece_basis.T,
        piece_basis,
        precision=lax.Precision.HIGHEST,
        preferred_element_type=jnp.float32,
    )
    gram_matrix = next_gram
    gram_matrix = gram_matrix + RIDGE * tile_count * jnp.eye(term_count, dtype=jnp.float32)
    factor = jnp.linalg.cholesky(gram_matrix)
    pupil_maps = jax.scipy.linalg.cho_solve(
        (factor, True), next_proj.reshape(term_count, -1)
    ).reshape(next_proj.shape)
    return jnp.einsum("tk,kcuv->tcuv", basis_rows, pupil_maps, precision=lax.Precision.HIGHEST)


def solution(mesh):
    placed = (
        P(("groups", "tile"), None, None, None),
        P(("groups", "tile"), None, None, None),
        P(("groups", "tile"), "led", None, None),
        P(("groups", "tile"), "led", None),
        P(("groups", "tile"), None),
    )
    return jax.shard_map(
        per_device,
        mesh=mesh,
        in_specs=placed,
        out_specs=P(("groups", "tile"), None, "led", None),
        check_vma=False,
    )
```

profile of v0, /device:TPU:0, one launch (start us, length us, event | category | flops | bytes accessed | tf_op | source)
XLA Modules:
  0.0 146.0 jit_solution(11602704741778709038)
XLA Ops:
  6.5 1.0 multiply_convert_fusion.4
  7.5 1.0 multiply_convert_fusion.2
  8.6 42.6 %while.59 = (s32[]{:T(128)}, f32[2,2,256,256]{3,2,1,0:T(8,128)}, f32[2]{0:T(128)S(1)}, bf16[2,2,256,256]{3,2,1,0:T(8,128)(2,1)}, s32[2,2,2]{2,1,0:T(2,128)}, /*i...) while((s32[]{:T(128)}, f32[2,2,256,256]{3,2,1,0:T(8,128)}, ...), condition=%wide.region_6.7_spmd, body=%wide.region_2.6_spmd.sunk | while | flops 542179328 | bytes 20447872 | solution.py:100
  8.7 0.7 fusion.78
  9.3 1.0 constant_dynamic-slice_fusion.5
  10.4 1.1 dynamic-slice_bitcast_fusion.5
  11.5 1.1 dynamic-slice_bitcast_fusion.4
  12.7 16.3 %while.60 = (s32[]{:T(128)}, f32[2,256,256]{2,1,0:T(8,128)S(1)}, f32[]{:T(128)}, s32[2,2]{1,0:T(2,128)S(1)}, bf16[2,384,384]{2,1,0:T(8,128)(2,1)S(1)}, /*index=5...) while((s32[]{:T(128)}, f32[2,256,256]{2,1,0:T(8,128)S(1)}, ...), condition=%wide.region_5.5_spmd.clone, body=%wide.region_3.4_spmd.clone.sunk | while | flops 542179328 | bytes 16122139 | solution.py:70
  12.7 0.7 fusion.87
  18.0 0.3 fusion.90
  18.5 0.3 convolution_bitcast_fusion.5
  19.2 0.8 add_bitcast_fusion.2
  20.9 0.7 fusion.87
  26.1 0.3 fusion.90
  26.6 0.3 convolution_bitcast_fusion.5
  27.3 0.8 add_bitcast_fusion.2
  29.1 0.8 bitcast_dynamic-update-slice_fusion.2
  29.9 0.7 fusion.78
  30.6 1.0 constant_dynamic-slice_fusion.5
  31.7 1.1 dynamic-slice_bitcast_fusion.5
  32.8 1.1 dynamic-slice_bitcast_fusion.4
  34.0 16.3 %while.60 = (s32[]{:T(128)}, f32[2,256,256]{2,1,0:T(8,128)S(1)}, f32[]{:T(128)}, s32[2,2]{1,0:T(2,128)S(1)}, bf16[2,384,384]{2,1,0:T(8,128)(2,1)S(1)}, /*index=5...) while((s32[]{:T(128)}, f32[2,256,256]{2,1,0:T(8,128)S(1)}, ...), condition=%wide.region_5.5_spmd.clone, body=%wide.region_3.4_spmd.clone.sunk | while | flops 542179328 | bytes 16122139 | solution.py:70
  34.0 0.7 fusion.87
  38.9 0.3 convolution_bitcast_fusion.4
  39.2 0.4 fusion.90
  39.8 0.3 convolution_bitcast_fusion.5
  40.5 0.8 add_bitcast_fusion.2
  42.1 0.7 fusion.87
  47.0 0.3 convolution_bitcast_fusion.4
  47.4 0.3 fusion.90
  47.9 0.3 convolution_bitcast_fusion.5
  48.6 0.8 add_bitcast_fusion.2
  50.4 0.8 bitcast_dynamic-update-slice_fusion.2
  51.3 13.5 %psum.15 = f32[2]{0:T(128)S(1)} all-reduce(f32[2]{0:T(128)S(1)} %get-tuple-element.572), channel_id=1, replica_groups=mesh['groups'=2,'tile'=4,'led'=4] {'led'}, use_global_device_ids=true, to_apply=%region_8.9 | all-reduce | flops 2 | bytes 16 | tf_op jit(solution)/shard_map/psum | solution.py:107
  64.8 41.2 %all-reduce.2.cloned.1.call-done = f32[2,2,256,256]{3,2,1,0:T(8,128)} async-done(((f32[2,2,256,256]{3,2,1,0:T(8,128)}), f32[2,2,256,256]{3,2,1,0:T(8,128)}) %all-reduce.2.cloned.1.call-update) | async-done | bytes 1048592 | tf_op jit(solution)/shard_map/psum | solution.py:107
  106.0 1.8 %divide_add_fusion = f32[2,2,64,256]{3,2,1,0:T(8,128)} fusion(f32[2,2,256,256]{3,2,1,0:T(8,128)} %all-reduce.2.cloned.1.call-done, s32[]{:T(128)S(6)} %select_n.48, f32[2,2,256,256]{3,2,1,0:T(8,128)} %get-tuple-element.1015, f32[2]{0:T(128)S(1)} %broadcast_multiply_fusion.4), kind=kLoop, calls=%fused_computation.72 | loop fusion | flops 131072 | bytes 786444 | tf_op jit(solution)/shard_map/add | solution.py:110
  108.2 5.2 %all-gather = f32[4,2,21]{2,1,0:T(2,128)S(1)} all-gather(f32[1,2,21]{2,1,0:T(2,128)S(1)} %bitcast.169), channel_id=1, replica_groups=mesh['groups'=2,'tile'=4,'led'=4] {'tile'}, dimensions={0}, use_global_device_ids=true | all-gather | bytes 840 | tf_op jit(solution)/shard_map/all_gather | solution.py:115
  113.8 1.9 %cholesky.16 = f32[21,21]{1,0:T(8,128)S(1)} custom-call(f32[21,21]{1,0:T(8,128)S(1)} %fusion.44), custom_call_target="Cholesky" | custom-call | tf_op jit(solution)/shard_map/jit(cholesky)/cholesky | solution.py:127
  115.7 0.7 compare_reduce_fusion
  116.4 0.6 fusion.39
  117.0 1.6 %custom-call.10 = f32[1,21,21]{1,2,0:T(8,128)S(1)} custom-call(f32[1,21,21]{2,1,0:T(8,128)S(1)} %fusion.39), custom_call_target="InvertDiagBlocksLowerTriangular" | custom-call | tf_op jit(solution)/shard_map/jit(_cho_solve)/triangular_solve | solution.py:128
  118.6 5.5 %all-gather.3.cloned.1.call-done = f32[8,2,64,256]{3,2,1,0:T(8,128)} async-done(((f32[2,2,64,256]{3,2,1,0:T(8,128)}), f32[8,2,64,256]{3,2,1,0:T(8,128)}) %all-gather.3.cloned.1.call-update) | async-done | bytes 1048592 | tf_op jit(solution)/shard_map/all_gather | solution.py:114
  124.1 4.2 %fusion.30 = f32[21,2,64,256]{3,0,2,1:T(8,128)S(1)} fusion(f32[8,21,1,1]{1,0,3,2:T(8,128)S(1)} %bitcast.168, f32[8,2,64,256]{3,2,1,0:T(8,128)} %all-gather.3.cloned.1.call-done), kind=kOutput, calls=%fused_computation.60 | convolution fusion | flops 66060288 | bytes 3801760 | tf_op jit(solution)/shard_map/tk,tcuv->kcuv/dot_general | solution.py:116
  128.3 0.9 copy.37
  129.2 4.6 %fusion.28 = f32[2,64,256,21]{2,3,1,0:T(8,128)S(1)} fusion(f32[2,64,256,21]{2,1,0,3:T(8,128)S(1)} %bitcast.166, f32[1,21,21]{1,2,0:T(8,128)S(1)} %custom-call.10), kind=kOutput, calls=%fused_computation.58 | convolution fusion | flops 173408256 | bytes 5506788 | tf_op jit(solution)/shard_map/jit(_cho_solve)/triangular_solve | solution.py:128
  133.8 2.8 %fusion.41 = f32[21,2,64,256]{3,0,2,1:T(8,128)S(1)} fusion(f32[2,64,256,21]{2,3,1,0:T(8,128)S(1)} %fusion.28, f32[1,21,21]{1,2,0:T(8,128)S(1)} %custom-call.10), kind=kOutput, calls=%fused_computation.83 | convolution fusion | flops 173408256 | bytes 5506788 | tf_op jit(solution)/shard_map/jit(_cho_solve)/triangular_solve | solution.py:128
  136.6 1.8 %fusion.47 = f32[2,2,64,256]{3,0,2,1:T(2,128)S(1)} fusion(f32[21,2,64,256]{3,0,2,1:T(8,128)S(1)} %fusion.41, f32[2,21]{1,0:T(2,128)S(1)} %stack.45), kind=kOutput, calls=%fused_computation.97 | convolution fusion | flops 16515072 | bytes 3014824 | tf_op jit(solution)/shard_map/tk,kcuv->tcuv/dot_general | solution.py:131
  138.4 0.7 copy.23
  (61 shorter events, 6.0 us)
Async XLA Ops:
  6.5 99.4 %all-reduce.2.cloned.1.call-start = ((), (), s32[]{:S(2)}) async-start(), calls=%async_computation | async-start | bytes 2097152 | tf_op jit(solution)/shard_map/psum | solution.py:107
  8.6 56.2 %copy-start = (s32[2,2]{1,0:T(2,128)S(1)}, s32[2,2]{1,0:T(2,128)}, u32[]{:S(2)}) copy-start(s32[2,2]{1,0:T(2,128)} %param.13) | copy-start | bytes 52
  51.3 72.9 %all-gather.3.cloned.1.call-start = ((), (), s32[]{:S(2)}) async-start(), calls=%async_computation.1 | async-start | bytes 1310720 | tf_op jit(solution)/shard_map/all_gather | solution.py:114
Sparse Core Ops, SparseCore 0:
  51.4 54.5 all-reduce.1
  108.0 16.1 all-gather.2
where the time goes:
time: 147 us; the launch traced here: 146 us
  waiting for transfers between devices  46.7 us (32%)
  loops' own time  19 us (13%)
  blocking collectives  18.7 us (13%)
  matrix products  18.6 us (13%)
  other arithmetic  15 us (10%)
  local copies, waits for them, and re-layouts  14.4 us (10%)
  between operations  13.5 us (9%)
    psum x1, waiting for transfers between devices, per_device(): grad_total, peak_total = lax.psum((gradient, peak_sums), 'led')  41.2 us
    another operation x2, loops' own time, tile_pass(): lax.scan(advance, start_state, (amplitude_set, offset_set))  18.9 us
    psum x1, blocking collectives, per_device(): grad_total, peak_total = lax.psum((gradient, peak_sums), 'led')  13.5 us
    another operation x2, matrix products, per_device(): jax.scipy.linalg.cho_solve((factor, True), next_proj.reshape(term_count,...  7.41 us
    squeeze x6, local copies, waits for them, and re-layouts, per_device(): lax.map(lambda items: tile_pass(items[0], items[1], items[2], items[3], t...  5.79 us
    all_gather x1, waiting for transfers between devices, per_device(): piece_rows = lax.all_gather(updated, 'tile', axis=0, tiled=True)  5.5 us
    all_gather x1, blocking collectives, per_device(): piece_basis = lax.all_gather(basis_rows, 'tile', axis=0, tiled=True)  5.25 us
    dot_general x16, matrix products, fourier_square(): jnp.dot(left_side, right_side, preferred_element_type=jnp.float32)  5.03 us
  transfers between devices with their start and end apart: 2, of which 2 were waited for; matrix products, arithmetic and copies ran while one was open for 4% of the time, Pallas kernels for 0%

commit v1 on v0

v1 whole, which is shorter than its diff:
```python
import functools
import math

import jax
import jax.numpy as jnp
import numpy as np
from jax import lax
from jax.experimental import pallas as pl
from jax.experimental.pallas import tpu as pltpu
from jax.sharding import PartitionSpec as P

DEG = 5
FIELD = 2048
RIDGE = 0.05
FLOOR = 0.25
MESH = pl.DeviceIdType.MESH


def inverse_tables(length):
    index = np.arange(length, dtype=np.int64)
    angle = (index[:, None] * index[None, :] % length) * (2.0 * math.pi / length)
    factor = 1.0 / math.sqrt(length)
    real_part = (np.cos(angle) * factor).astype(np.float32)
    imag_part = (np.sin(angle) * factor).astype(np.float32)
    first = np.block([[real_part, -imag_part], [imag_part, real_part]])
    second = np.block([[real_part, imag_part], [-imag_part, real_part]])
    return first.astype(jnp.bfloat16), second.astype(jnp.bfloat16)


def legendre(values):
    polys = [jnp.ones_like(values), values]
    for degree in range(2, DEG + 1):
        polys.append(((2 * degree - 1) * values * polys[-1] - (degree - 1) * polys[-2]) / degree)
    return polys


def mixing_matrix(place_rows, tiles):
    lanes = lax.broadcasted_iota(jnp.int32, (tiles, 128), 1)
    subs = lax.broadcasted_iota(jnp.int32, (tiles, 128), 0)
    ridge = RIDGE * tiles
    products = []
    for axis in range(2):
        down = jnp.zeros((tiles, 128), jnp.float32)
        along = jnp.zeros((tiles, 128), jnp.float32)
        for tile in range(tiles):
            row = jnp.broadcast_to(place_rows[tile][axis], (tiles, 128))
            down = jnp.where(subs == tile, row, down)
            along = jnp.where(lanes == tile, row, along)
        scale = 2.0 / (FIELD - 1)
        down, along = (down * scale - 1.0, along * scale - 1.0)
        products.append([a * b for a, b in zip(legendre(down), legendre(along))])
    kernel = jnp.zeros((tiles, 128), jnp.float32)
    partial = jnp.zeros((tiles, 128), jnp.float32)
    for degree in range(DEG + 1):
        partial = partial + products[1][degree]
        kernel = kernel + products[0][DEG - degree] * partial
    eye = jnp.where(subs == lanes, 1.0, 0.0)
    left = kernel + ridge * eye
    right = eye
    for step in range(tiles):
        pivot_row = left[step : step + 1, :]
        pivot = jnp.sum(jnp.where(lanes[:1] == step, pivot_row, 0.0), axis=1, keepdims=True)
        column = jnp.sum(jnp.where(lanes == step, left, 0.0), axis=1, keepdims=True)
        factor = jnp.where(subs[:, :1] == step, 1.0 - 1.0 / pivot, column / pivot)
        left = left - factor * pivot_row
        right = right - factor * right[step : step + 1, :]
    return eye - ridge * right


def pick(count, size, at, flip):
    shape = (size, count) if flip else (count, size)
    down = lax.broadcasted_iota(jnp.int32, shape, 0)
    along = lax.broadcasted_iota(jnp.int32, shape, 1)
    gap = down - along if flip else along - down
    return jnp.where(gap == at, 1.0, 0.0).astype(jnp.bfloat16)


def windows(planes, a, b, length):
    size = planes.shape[1]
    lanes = pick(length, size, b, True)
    narrow = jnp.dot(planes.reshape(2 * size, size), lanes, preferred_element_type=jnp.float32)
    narrow = narrow.astype(jnp.bfloat16)
    both = jnp.concatenate([narrow[:size], narrow[size:]], 1)
    both = jnp.dot(pick(length, size, a, False), both, preferred_element_type=jnp.float32)
    return both[:, :length], both[:, length:]


def kernel(
    n, m, led_total,
    spectra_ref, pupils_ref, amps_ref, offsets_ref, positions_ref, first_ref, second_ref,
    out_ref,
    stack, wide, grad, from_left, from_right, peaks, places, gathered,
    peak_send, peak_recv, place_send, place_recv,
    right_send, right_recv, left_send, left_recv, tile_send, tile_recv,
):
    tl, leds = amps_ref.shape[0], amps_ref.shape[1]
    length = pupils_ref.shape[2]
    rows = length // n
    z = lax.axis_index("led")
    me = lax.axis_index("tile")
    tiles = tl * m

    def led_peer(d):
        return {"led": lax.rem(z + d, n)}

    def tile_peer(d):
        return {"tile": lax.rem(me + d, m)}

    def strip(q):
        return pl.ds(pl.multiple_of(q * rows, rows), rows)

    barrier = pltpu.get_barrier_semaphore()
    for d in range(1, n):
        pl.semaphore_signal(barrier, inc=1, device_id=led_peer(d), device_id_type=MESH)
    for d in range(1, m):
        pl.semaphore_signal(barrier, inc=1, device_id=tile_peer(d), device_id_type=MESH)

    subs = lax.broadcasted_iota(jnp.int32, (8, 128), 0)

    place = jnp.zeros((8, 128), jnp.float32)
    for t in range(tl):
        for axis in range(2):
            value = positions_ref[t, axis].astype(jnp.float32)
            place = jnp.where(subs == 2 * t + axis, value, place)
    places[0] = place

    def place_copy(d):
        return pltpu.make_async_remote_copy(
            places.at[0], places.at[d], place_send.at[d], place_recv.at[d],
            device_id=tile_peer(d), device_id_type=MESH)

    def peak_copy(d):
        return pltpu.make_async_remote_copy(
            peaks.at[0], peaks.at[d], peak_send.at[d], peak_recv.at[d],
            device_id=led_peer(d), device_id_type=MESH)

    def right_copy(t, c, q):
        return pltpu.make_async_remote_copy(
            grad.at[t, c, strip(q)], from_left.at[t, c, q],
            right_send.at[t, c, q], right_recv.at[t, c, q],
            device_id=led_peer(1), device_id_type=MESH)

    def left_copy(t, c, q):
        return pltpu.make_async_remote_copy(
            grad.at[t, c, strip(q)], from_right.at[t, c, q],
            left_send.at[t, c, q], left_recv.at[t, c, q],
            device_id=led_peer(n - 1), device_id_type=MESH)

    def tile_copy(t, c, d):
        return pltpu.make_async_remote_copy(
            gathered.at[me, t, c], gathered.at[me, t, c],
            tile_send.at[t, c, d], tile_recv.at[t, c, d],
            device_id=tile_peer(d), device_id_type=MESH)

    def tile_arrival(t, c, d):
        source = lax.rem(me + m - d, m)
        return pltpu.make_async_remote_copy(
            gathered.at[me, t, c], gathered.at[source, t, c],
            tile_send.at[t, c, d], tile_recv.at[t, c, d],
            device_id=tile_peer(d), device_id_type=MESH)

    def work(t):
        peak = jnp.zeros((1, 1), jnp.float32)
        for led in range(leds):
            a = offsets_ref[t, led, 0]
            b = offsets_ref[t, led, 1]
            window_re, window_im = windows(spectra_ref[t], a, b, length)
            pupil_re, pupil_im = (pupils_ref[t, 0], pupils_ref[t, 1])
            power = window_re * window_re + window_im * window_im
            power = jnp.max(jnp.max(power, axis=0, keepdims=True), axis=1, keepdims=True)
            peak = peak + power
            stack[led, :length] = (pupil_re * window_re - pupil_im * window_im).astype(jnp.bfloat16)
            stack[led, length:] = (pupil_re * window_im + pupil_im * window_re).astype(jnp.bfloat16)
            inner = jnp.dot(first_ref[...], stack[led], preferred_element_type=jnp.float32)
            wide[led, :, :length] = inner[:length].astype(jnp.bfloat16)
            wide[led, :, length:] = inner[length:].astype(jnp.bfloat16)
            wave = jnp.dot(wide[led], second_ref[...], preferred_element_type=jnp.float32)
            wave_re, wave_im = (wave[:, :length], wave[:, length:])
            squared = jnp.maximum(wave_re * wave_re + wave_im * wave_im, FLOOR * FLOOR)
            ratio = amps_ref[t, led].astype(jnp.float32) * lax.rsqrt(squared) - 1.0
            stack[led, :length] = (wave_re * ratio).astype(jnp.bfloat16)
            stack[led, length:] = (wave_im * ratio).astype(jnp.bfloat16)
            inner = jnp.dot(second_ref[...], stack[led], preferred_element_type=jnp.float32)
            wide[led, :, :length] = inner[:length].astype(jnp.bfloat16)
            wide[led, :, length:] = inner[length:].astype(jnp.bfloat16)
            delta = jnp.dot(wide[led], first_ref[...], preferred_element_type=jnp.float32)
            delta_re, delta_im = (delta[:, :length], delta[:, length:])
            grad_re = window_re * delta_re + window_im * delta_im
            grad_im = window_re * delta_im - window_im * delta_re
            if led == 0:
                grad[t, 0] = grad_re
                grad[t, 1] = grad_im
            else:
                grad[t, 0] += grad_re
                grad[t, 1] += grad_im
        peaks[0, t] = jnp.broadcast_to(peak, (8, 128))

    pl.semaphore_wait(barrier, n - 1 + m - 1)
    for d in range(1, m):
        place_copy(d).start()

    for t in range(tl):
        work(t)

        @pl.when(z == 0)
        def _():
            for q in range(n - 1, 0, -1):
                for c in range(2):
                    right_copy(t, c, q).start()

        @pl.when(z == n - 1)
        def _():
            for q in range(n - 1):
                for c in range(2):
                    left_copy(t, c, q).start()

    for d in range(1, n):
        peak_copy(d).start()
    for d in range(1, m):
        place_copy(d).wait_recv()
    place_rows = [None] * tiles
    for d in range(m):
        for t in range(tl):
            place_rows[d * tl + t] = (places[d, 2 * t : 2 * t + 1, :], places[d, 2 * t + 1 : 2 * t + 2, :])
    mix = mixing_matrix(place_rows, tiles)
    for d in range(1, n):
        peak_copy(d).wait_recv()

    for t in range(tl):
        peak = peaks[0, t]
        for d in range(1, n):
            peak = peak + peaks[d, t]
        mean_peak = jnp.broadcast_to((peak / led_total)[:1, :1], (rows, length))
        for d in range(n - 1, 0, -1):
            for c in range(2):
                @pl.when(jnp.logical_and(z > 0, z + d < n))
                def _():
                    q = z + d
                    right_copy(t, c, q).wait_recv()
                    grad[t, c, strip(q)] += from_left[t, c, q]
                    right_copy(t, c, q).start()

                @pl.when(jnp.logical_and(z < n - 1, z - d >= 0))
                def _():
                    q = z - d
                    left_copy(t, c, q).wait_recv()
                    grad[t, c, strip(q)] += from_right[t, c, q]
                    left_copy(t, c, q).start()
        for c in range(2):
            @pl.when(z > 0)
            def _():
                right_copy(t, c, z).wait_recv()
                grad[t, c, strip(z)] += from_left[t, c, z]

            @pl.when(z < n - 1)
            def _():
                left_copy(t, c, z).wait_recv()
                grad[t, c, strip(z)] += from_right[t, c, z]

            gathered[me, t, c] = pupils_ref[t, c, strip(z)] + grad[t, c, strip(z)] / mean_peak
            for d in range(1, m):
                tile_copy(t, c, d).start()

    for t in range(tl):
        for c in range(2):
            totals = [jnp.zeros((rows, length), jnp.float32) for _ in range(tl)]
            for d in range(m):
                if d:
                    tile_arrival(t, c, d).wait_recv()
                piece = gathered[lax.rem(me + m - d, m), t, c]
                at = d * tl + t
                for own in range(tl):
                    totals[own] += jnp.broadcast_to(mix[own : own + 1, at : at + 1], (rows, length)) * piece
            for own in range(tl):
                if t == 0:
                    out_ref[own, c] = totals[own]
                else:
                    out_ref[own, c] += totals[own]

    for d in range(1, m):
        place_copy(d).wait_send()
    for d in range(1, n):
        peak_copy(d).wait_send()
    for t in range(tl):
        for c in range(2):
            for d in range(1, m):
                tile_copy(t, c, d).wait_send()
            for d in range(1, n):
                @pl.when(z + d < n)
                def _():
                    right_copy(t, c, z + d).wait_send()

                @pl.when(z - d >= 0)
                def _():
                    left_copy(t, c, z - d).wait_send()


def per_device(n, m, spectra, pupils, amplitudes, offsets, positions):
    tl, leds = amplitudes.shape[:2]
    length = pupils.shape[2]
    rows = length // n
    first, second = inverse_tables(length)
    vmem = pl.BlockSpec(memory_space=pltpu.VMEM)
    smem = pl.BlockSpec(memory_space=pltpu.SMEM)
    dma = pltpu.SemaphoreType.DMA
    strips = pltpu.VMEM((tl, 2, n, rows, length), jnp.float32)
    return pl.pallas_call(
        functools.partial(kernel, n, m, leds * n),
        out_shape=jax.ShapeDtypeStruct((tl, 2, rows, length), jnp.float32),
        in_specs=[vmem, vmem, vmem, smem, smem, vmem, vmem],
        out_specs=vmem,
        scratch_shapes=[
            pltpu.VMEM((leds, 2 * length, length), jnp.bfloat16),
            pltpu.VMEM((leds, length, 2 * length), jnp.bfloat16),
            pltpu.VMEM((tl, 2, length, length), jnp.float32),
            strips,
            strips,
            pltpu.VMEM((n, tl, 8, 128), jnp.float32),
            pltpu.VMEM((m, 8, 128), jnp.float32),
            pltpu.VMEM((m, tl, 2, rows, length), jnp.float32),
            dma((n,)), dma((n,)), dma((m,)), dma((m,)),
            dma((tl, 2, n)), dma((tl, 2, n)), dma((tl, 2, n)), dma((tl, 2, n)),
            dma((tl, 2, m)), dma((tl, 2, m)),
        ],
        compiler_params=pltpu.CompilerParams(
            collective_id=0, has_side_effects=True, vmem_limit_bytes=40 << 20
        ),
    )(spectra, pupils, amplitudes, offsets, positions, jnp.asarray(first), jnp.asarray(second))


def solution(mesh):
    placed = (
        P(("groups", "tile"), None, None, None),
        P(("groups", "tile"), None, None, None),
        P(("groups", "tile"), "led", None, None),
        P(("groups", "tile"), "led", None),
        P(("groups", "tile"), None),
    )
    return jax.shard_map(
        functools.partial(per_device, mesh.shape["led"], mesh.shape["tile"]),
        mesh=mesh,
        in_specs=placed,
        out_specs=P(("groups", "tile"), None, "led", None),
        check_vma=False,
    )
```

time: 147 us -> 57.4 us (0.39)
  Pallas kernels: 0 us -> 49.3 us
  waiting for transfers between devices: 46.7 us -> 0 us
  loops' own time: 19 us -> 0 us
  blocking collectives: 18.7 us -> 0 us
  matrix products: 18.6 us -> 0 us
  other arithmetic: 15 us -> 0 us
  between operations: 13.5 us -> 0.02 us
  local copies, waits for them, and re-layouts: 14.4 us -> 7.68 us
    pallas_call x0 -> x1, Pallas kernels: none -> 49.3 us  [per_device(): pl.pallas_call(functools.partial(kernel, n, m, leds * n), out_shape=jax.S...]
    psum x1 -> x0, waiting for transfers between devices: 41.2 us -> none  [per_device(): grad_total, peak_total = lax.psum((gradient, peak_sums), 'led')]
    another operation x3 -> x0, loops' own time: 19 us -> none  [the longest x2 18.9 us: tile_pass(): lax.scan(advance, start_state, (amplitude_set, offset_set))]
    psum x1 -> x0, blocking collectives: 13.5 us -> none  [per_device(): grad_total, peak_total = lax.psum((gradient, peak_sums), 'led')]
    dot_general x19 -> x0, matrix products: 11.2 us -> none  [the longest x16 5.03 us: fourier_square(): jnp.dot(left_side, right_side, preferred_element_type=jnp.float32)]
    another operation x10 -> x0, other arithmetic: 8.01 us -> none  [the longest x4 3.15 us: led_update(): return (jnp.stack([grad_re, grad_im]), peak_value)]
    unnamed x2 -> x15, local copies, waits for them, and re-layouts: 0.01 us -> 7.68 us
    another operation x2 -> x0, matrix products: 7.41 us -> none  [per_device(): jax.scipy.linalg.cho_solve((factor, True), next_proj.reshape(term_count,...]
  transfers between devices with their start and end apart: 2 -> 0, of which waited for: 2 -> 0; matrix products, arithmetic and copies ran while one was open for 4% -> 0% of each run, Pallas kernels for 0% -> 0%
where the time goes in v1:
time: 57.4 us; the launch traced here: 57 us
  Pallas kernels  49.3 us (86%)
  local copies, waits for them, and re-layouts  7.68 us (13%)
    pallas_call x1, Pallas kernels, per_device(): pl.pallas_call(functools.partial(kernel, n, m, leds * n), out_shape=jax.S...  49.3 us
    unnamed x15, local copies, waits for them, and re-layouts  7.68 us

profile of v1, /device:TPU:0, one launch (start us, length us, event | category | flops | bytes accessed | tf_op | source)
XLA Modules:
  0.0 57.0 jit_solution(4832787313451991197)
XLA Ops:
  0.0 0.0 copy-start
  0.0 1.3 %copy-done = bf16[2,2,384,384]{3,2,1,0:T(8,128)(2,1)S(1)} copy-done((bf16[2,2,384,384]{3,2,1,0:T(8,128)(2,1)S(1)}, bf16[2,2,384,384]{3,2,1,0:T(8,128)(2,1)}, u32[]{:S(2)}) %copy-start) | copy-done | bytes 1179672
  1.3 0.0 copy-start.1
  1.3 1.2 %copy-done.1 = f32[2,2,256,256]{3,2,1,0:T(8,128)S(1)} copy-done((f32[2,2,256,256]{3,2,1,0:T(8,128)S(1)}, f32[2,2,256,256]{3,2,1,0:T(8,128)}, u32[]{:S(2)}) %copy-start.1) | copy-done | bytes 1048600
  2.5 0.0 copy-start.2
  2.5 1.0 %copy-done.2 = bf16[2,2,256,256]{3,2,1,0:T(8,128)(2,1)S(1)} copy-done((bf16[2,2,256,256]{3,2,1,0:T(8,128)(2,1)S(1)}, bf16[2,2,256,256]{3,2,1,0:T(8,128)(2,1)}, u32[]{:S(2)}) %copy-start.2) | copy-done | bytes 524312
  3.5 0.0 copy-start.3
  3.5 1.0 %copy-done.3 = bf16[512,512]{1,0:T(8,128)(2,1)S(1)} copy-done((bf16[512,512]{1,0:T(8,128)(2,1)S(1)}, bf16[512,512]{1,0:T(8,128)(2,1)}, u32[]{:S(2)}) %copy-start.3) | copy-done | bytes 524312
  4.6 0.0 copy-start.4
  4.6 1.0 %copy-done.4 = bf16[512,512]{1,0:T(8,128)(2,1)S(1)} copy-done((bf16[512,512]{1,0:T(8,128)(2,1)S(1)}, bf16[512,512]{1,0:T(8,128)(2,1)}, u32[]{:S(2)}) %copy-start.4) | copy-done | bytes 524312
  5.6 0.0 copy-start.5
  5.6 0.7 %copy-done.5 = s32[2,2,2]{2,1,0:T(2,128)S(1)} copy-done((s32[2,2,2]{2,1,0:T(2,128)S(1)}, s32[2,2,2]{2,1,0:T(2,128)}, u32[]{:S(2)}) %copy-start.5) | copy-done | bytes 56
  6.3 0.0 copy-start.6
  6.3 0.7 %copy-done.6 = s32[2,2]{1,0:T(2,128)S(1)} copy-done((s32[2,2]{1,0:T(2,128)S(1)}, s32[2,2]{1,0:T(2,128)}, u32[]{:S(2)}) %copy-start.6) | copy-done | bytes 40
  7.0 49.3 %shard_map.73 = f32[2,2,64,256]{3,2,1,0:T(8,128)S(1)} custom-call(bf16[2,2,384,384]{3,2,1,0:T(8,128)(2,1)S(1)} %copy-done, f32[2,2,256,256]{3,2,1,0:T(8,128)S(1)} %copy-done.1, bf16[2,2,256,256]{3,2,1,0:T(8,128)(2,1)S(1)} %copy-done.2, s32[2,2,2]{2,1,0:T(2,128)S(1)} %copy-done.5, s32[2,2]{1,0:T(2,128)S(1)} %copy-done.6, bf16[512,512]{1,0:T(8,128)(2,1)S(1)} %copy-done.4, ...), custom_call_target="tpu_custom_call" | custom-call | tf_op jit(solution)/shard_map/pallas_call | solution.py:307
  56.3 0.7 %copy.9 = f32[2,2,64,256]{3,2,1,0:T(8,128)} copy(f32[2,2,64,256]{3,2,1,0:T(8,128)S(1)} %shard_map.73) | data formatting | bytes 524288
Async XLA Ops:
  0.0 1.3 %copy-start = (bf16[2,2,384,384]{3,2,1,0:T(8,128)(2,1)S(1)}, bf16[2,2,384,384]{3,2,1,0:T(8,128)(2,1)}, u32[]{:S(2)}) copy-start(bf16[2,2,384,384]{3,2,1,0:T(8,128)(2,1)} %spectra_ref.1) | copy-start | bytes 3538948
  1.3 1.2 %copy-start.1 = (f32[2,2,256,256]{3,2,1,0:T(8,128)S(1)}, f32[2,2,256,256]{3,2,1,0:T(8,128)}, u32[]{:S(2)}) copy-start(f32[2,2,256,256]{3,2,1,0:T(8,128)} %pupils_ref.1) | copy-start | bytes 3145732
  2.5 1.0 %copy-start.2 = (bf16[2,2,256,256]{3,2,1,0:T(8,128)(2,1)S(1)}, bf16[2,2,256,256]{3,2,1,0:T(8,128)(2,1)}, u32[]{:S(2)}) copy-start(bf16[2,2,256,256]{3,2,1,0:T(8,128)(2,1)} %amps_ref.1) | copy-start | bytes 1572868
  3.5 1.0 %copy-start.3 = (bf16[512,512]{1,0:T(8,128)(2,1)S(1)}, bf16[512,512]{1,0:T(8,128)(2,1)}, u32[]{:S(2)}) copy-start(bf16[512,512]{1,0:T(8,128)(2,1)} %constant.5.clone.second_ref) | copy-start | bytes 1572868
  4.6 1.0 %copy-start.4 = (bf16[512,512]{1,0:T(8,128)(2,1)S(1)}, bf16[512,512]{1,0:T(8,128)(2,1)}, u32[]{:S(2)}) copy-start(bf16[512,512]{1,0:T(8,128)(2,1)} %constant.4.clone.first_ref) | copy-start | bytes 1572868
  5.6 0.7 %copy-start.5 = (s32[2,2,2]{2,1,0:T(2,128)S(1)}, s32[2,2,2]{2,1,0:T(2,128)}, u32[]{:S(2)}) copy-start(s32[2,2,2]{2,1,0:T(2,128)} %offsets_ref.1) | copy-start | bytes 100
  6.3 0.7 %copy-start.6 = (s32[2,2]{1,0:T(2,128)S(1)}, s32[2,2]{1,0:T(2,128)}, u32[]{:S(2)}) copy-start(s32[2,2]{1,0:T(2,128)} %positions_ref.1) | copy-start | bytes 52

commit v2 on v1

--- a/solution.py
+++ b/solution.py
@@ -87,8 +87,9 @@
 
 def kernel(
     n, m, led_total,
-    spectra_ref, pupils_ref, amps_ref, offsets_ref, positions_ref, first_ref, second_ref,
+    spectra_hbm, pupils_hbm, amps_hbm, offsets_hbm, positions_hbm, first_hbm, second_hbm,
     out_ref,
+    spectra_ref, pupils_ref, amps_ref, offsets_ref, positions_ref, first_ref, second_ref, load_sem,
     stack, wide, grad, from_left, from_right, peaks, places, gathered,
     peak_send, peak_recv, place_send, place_recv,
     right_send, right_recv, left_send, left_recv, tile_send, tile_recv,
@@ -109,6 +110,22 @@
     def strip(q):
         return pl.ds(pl.multiple_of(q * rows, rows), rows)
 
+    loads = {}
+    for name, source, target in [
+        ("offsets", offsets_hbm, offsets_ref),
+        *[(("spectra", t), spectra_hbm.at[t], spectra_ref.at[t]) for t in range(1)],
+        *[(("pupils", t), pupils_hbm.at[t], pupils_ref.at[t]) for t in range(1)],
+        ("first", first_hbm, first_ref),
+        ("second", second_hbm, second_ref),
+        *[(("amps", t), amps_hbm.at[t], amps_ref.at[t]) for t in range(1)],
+        ("positions", positions_hbm, positions_ref),
+        *[(("spectra", t), spectra_hbm.at[t], spectra_ref.at[t]) for t in range(1, tl)],
+        *[(("pupils", t), pupils_hbm.at[t], pupils_ref.at[t]) for t in range(1, tl)],
+        *[(("amps", t), amps_hbm.at[t], amps_ref.at[t]) for t in range(1, tl)],
+    ]:
+        loads[name] = pltpu.make_async_copy(source, target, load_sem.at[len(loads)])
+        loads[name].start()
+
     barrier = pltpu.get_barrier_semaphore()
     for d in range(1, n):
         pl.semaphore_signal(barrier, inc=1, device_id=led_peer(d), device_id_type=MESH)
@@ -117,13 +134,6 @@
 
     subs = lax.broadcasted_iota(jnp.int32, (8, 128), 0)
 
-    place = jnp.zeros((8, 128), jnp.float32)
-    for t in range(tl):
-        for axis in range(2):
-            value = positions_ref[t, axis].astype(jnp.float32)
-            place = jnp.where(subs == 2 * t + axis, value, place)
-    places[0] = place
-
     def place_copy(d):
         return pltpu.make_async_remote_copy(
             places.at[0], places.at[d], place_send.at[d], place_recv.at[d],
@@ -160,23 +170,34 @@
             device_id=tile_peer(d), device_id_type=MESH)
 
     def work(t):
+        loads["spectra", t].wait()
+        if t == 0:
+            loads["offsets"].wait()
         peak = jnp.zeros((1, 1), jnp.float32)
         for led in range(leds):
             a = offsets_ref[t, led, 0]
             b = offsets_ref[t, led, 1]
             window_re, window_im = windows(spectra_ref[t], a, b, length)
+            if led == 0:
+                loads["pupils", t].wait()
             pupil_re, pupil_im = (pupils_ref[t, 0], pupils_ref[t, 1])
             power = window_re * window_re + window_im * window_im
             power = jnp.max(jnp.max(power, axis=0, keepdims=True), axis=1, keepdims=True)
             peak = peak + power
             stack[led, :length] = (pupil_re * window_re - pupil_im * window_im).astype(jnp.bfloat16)
             stack[led, length:] = (pupil_re * window_im + pupil_im * window_re).astype(jnp.bfloat16)
+            if t == 0 and led == 0:
+                loads["first"].wait()
             inner = jnp.dot(first_ref[...], stack[led], preferred_element_type=jnp.float32)
             wide[led, :, :length] = inner[:length].astype(jnp.bfloat16)
             wide[led, :, length:] = inner[length:].astype(jnp.bfloat16)
+            if t == 0 and led == 0:
+                loads["second"].wait()
             wave = jnp.dot(wide[led], second_ref[...], preferred_element_type=jnp.float32)
             wave_re, wave_im = (wave[:, :length], wave[:, length:])
             squared = jnp.maximum(wave_re * wave_re + wave_im * wave_im, FLOOR * FLOOR)
+            if led == 0:
+                loads["amps", t].wait()
             ratio = amps_ref[t, led].astype(jnp.float32) * lax.rsqrt(squared) - 1.0
             stack[led, :length] = (wave_re * ratio).astype(jnp.bfloat16)
             stack[led, length:] = (wave_im * ratio).astype(jnp.bfloat16)
@@ -195,12 +216,11 @@
                 grad[t, 1] += grad_im
         peaks[0, t] = jnp.broadcast_to(peak, (8, 128))
 
-    pl.semaphore_wait(barrier, n - 1 + m - 1)
-    for d in range(1, m):
-        place_copy(d).start()
 
     for t in range(tl):
         work(t)
+        if t == 0:
+            pl.semaphore_wait(barrier, n - 1 + m - 1)
 
         @pl.when(z == 0)
         def _():
@@ -216,6 +236,16 @@
 
     for d in range(1, n):
         peak_copy(d).start()
+    loads["positions"].wait()
+    place = jnp.zeros((8, 128), jnp.float32)
+    for t in range(tl):
+        for axis in range(2):
+            value = positions_ref[t, axis].astype(jnp.float32)
+            place = jnp.where(subs == 2 * t + axis, value, place)
+    places[0] = place
+
+    for d in range(1, m):
+        place_copy(d).start()
     for d in range(1, m):
         place_copy(d).wait_recv()
     place_rows = [None] * tiles
@@ -299,17 +329,23 @@
     tl, leds = amplitudes.shape[:2]
     length = pupils.shape[2]
     rows = length // n
-    first, second = inverse_tables(length)
     vmem = pl.BlockSpec(memory_space=pltpu.VMEM)
-    smem = pl.BlockSpec(memory_space=pltpu.SMEM)
+    hbm = pl.BlockSpec(memory_space=pltpu.HBM)
+    first, second = (jnp.asarray(table) for table in inverse_tables(length))
+    operands = (spectra, pupils, amplitudes, offsets, positions, first, second)
     dma = pltpu.SemaphoreType.DMA
     strips = pltpu.VMEM((tl, 2, n, rows, length), jnp.float32)
     return pl.pallas_call(
         functools.partial(kernel, n, m, leds * n),
         out_shape=jax.ShapeDtypeStruct((tl, 2, rows, length), jnp.float32),
-        in_specs=[vmem, vmem, vmem, smem, smem, vmem, vmem],
+        in_specs=[hbm] * 7,
         out_specs=vmem,
         scratch_shapes=[
+            *[
+                (pltpu.SMEM if each.dtype == jnp.int32 else pltpu.VMEM)(each.shape, each.dtype)
+                for each in operands
+            ],
+            dma((4 + 3 * tl,)),
             pltpu.VMEM((leds, 2 * length, length), jnp.bfloat16),
             pltpu.VMEM((leds, length, 2 * length), jnp.bfloat16),
             pltpu.VMEM((tl, 2, length, length), jnp.float32),
@@ -325,7 +361,7 @@
         compiler_params=pltpu.CompilerParams(
             collective_id=0, has_side_effects=True, vmem_limit_bytes=40 << 20
         ),
-    )(spectra, pupils, amplitudes, offsets, positions, jnp.asarray(first), jnp.asarray(second))
+    )(*operands)
 
 
 def solution(mesh):

time: 57.4 us -> 56.4 us (0.983)
  Pallas kernels: 49.3 us -> 47.7 us
    pallas_call x1, Pallas kernels: 49.3 us -> 47.7 us  [per_device(): pl.pallas_call(functools.partial(kernel, n, m, leds * n), out_shape=jax.S...]
where the time goes in v2:
time: 56.4 us; the launch traced here: 55.4 us
  Pallas kernels  47.7 us (85%)
  local copies, waits for them, and re-layouts  7.68 us (14%)
    pallas_call x1, Pallas kernels, per_device(): pl.pallas_call(functools.partial(kernel, n, m, leds * n), out_shape=jax.S...  47.7 us
    unnamed x15, local copies, waits for them, and re-layouts  7.68 us

profile of v2, /device:TPU:0, one launch (start us, length us, event | category | flops | bytes accessed | tf_op | source)
XLA Modules:
  0.0 55.4 jit_solution(10612272927559038616)
XLA Ops:
  0.0 0.0 copy-start
  0.0 1.3 %copy-done = bf16[2,2,384,384]{3,2,1,0:T(8,128)(2,1)S(1)} copy-done((bf16[2,2,384,384]{3,2,1,0:T(8,128)(2,1)S(1)}, bf16[2,2,384,384]{3,2,1,0:T(8,128)(2,1)}, u32[]{:S(2)}) %copy-start) | copy-done | bytes 1179672
  1.3 0.0 copy-start.1
  1.3 1.2 %copy-done.1 = f32[2,2,256,256]{3,2,1,0:T(8,128)S(1)} copy-done((f32[2,2,256,256]{3,2,1,0:T(8,128)S(1)}, f32[2,2,256,256]{3,2,1,0:T(8,128)}, u32[]{:S(2)}) %copy-start.1) | copy-done | bytes 1048600
  2.5 0.0 copy-start.2
  2.5 1.0 %copy-done.2 = bf16[2,2,256,256]{3,2,1,0:T(8,128)(2,1)S(1)} copy-done((bf16[2,2,256,256]{3,2,1,0:T(8,128)(2,1)S(1)}, bf16[2,2,256,256]{3,2,1,0:T(8,128)(2,1)}, u32[]{:S(2)}) %copy-start.2) | copy-done | bytes 524312
  3.5 0.0 copy-start.3
  3.5 1.0 %copy-done.3 = bf16[512,512]{1,0:T(8,128)(2,1)S(1)} copy-done((bf16[512,512]{1,0:T(8,128)(2,1)S(1)}, bf16[512,512]{1,0:T(8,128)(2,1)}, u32[]{:S(2)}) %copy-start.3) | copy-done | bytes 524312
  4.6 0.0 copy-start.4
  4.6 1.0 %copy-done.4 = bf16[512,512]{1,0:T(8,128)(2,1)S(1)} copy-done((bf16[512,512]{1,0:T(8,128)(2,1)S(1)}, bf16[512,512]{1,0:T(8,128)(2,1)}, u32[]{:S(2)}) %copy-start.4) | copy-done | bytes 524312
  5.6 0.0 copy-start.5
  5.6 0.7 %copy-done.5 = s32[2,2,2]{2,1,0:T(2,128)S(1)} copy-done((s32[2,2,2]{2,1,0:T(2,128)S(1)}, s32[2,2,2]{2,1,0:T(2,128)}, u32[]{:S(2)}) %copy-start.5) | copy-done | bytes 56
  6.3 0.0 copy-start.6
  6.3 0.7 %copy-done.6 = s32[2,2]{1,0:T(2,128)S(1)} copy-done((s32[2,2]{1,0:T(2,128)S(1)}, s32[2,2]{1,0:T(2,128)}, u32[]{:S(2)}) %copy-start.6) | copy-done | bytes 40
  7.0 47.7 %shard_map.73 = f32[2,2,64,256]{3,2,1,0:T(8,128)S(1)} custom-call(bf16[2,2,384,384]{3,2,1,0:T(8,128)(2,1)S(1)} %copy-done, f32[2,2,256,256]{3,2,1,0:T(8,128)S(1)} %copy-done.1, bf16[2,2,256,256]{3,2,1,0:T(8,128)(2,1)S(1)} %copy-done.2, s32[2,2,2]{2,1,0:T(2,128)S(1)} %copy-done.5, s32[2,2]{1,0:T(2,128)S(1)} %copy-done.6, bf16[512,512]{1,0:T(8,128)(2,1)S(1)} %copy-done.4, ...), custom_call_target="tpu_custom_call" | custom-call | tf_op jit(solution)/shard_map/pallas_call | solution.py:338
  54.7 0.7 %copy.9 = f32[2,2,64,256]{3,2,1,0:T(8,128)} copy(f32[2,2,64,256]{3,2,1,0:T(8,128)S(1)} %shard_map.73) | data formatting | bytes 524288
Async XLA Ops:
  0.0 1.3 %copy-start = (bf16[2,2,384,384]{3,2,1,0:T(8,128)(2,1)S(1)}, bf16[2,2,384,384]{3,2,1,0:T(8,128)(2,1)}, u32[]{:S(2)}) copy-start(bf16[2,2,384,384]{3,2,1,0:T(8,128)(2,1)} %spectra_hbm.1) | copy-start | bytes 3538948
  1.3 1.2 %copy-start.1 = (f32[2,2,256,256]{3,2,1,0:T(8,128)S(1)}, f32[2,2,256,256]{3,2,1,0:T(8,128)}, u32[]{:S(2)}) copy-start(f32[2,2,256,256]{3,2,1,0:T(8,128)} %pupils_hbm.1) | copy-start | bytes 3145732
  2.5 1.0 %copy-start.2 = (bf16[2,2,256,256]{3,2,1,0:T(8,128)(2,1)S(1)}, bf16[2,2,256,256]{3,2,1,0:T(8,128)(2,1)}, u32[]{:S(2)}) copy-start(bf16[2,2,256,256]{3,2,1,0:T(8,128)(2,1)} %amps_hbm.1) | copy-start | bytes 1572868
  3.5 1.0 %copy-start.3 = (bf16[512,512]{1,0:T(8,128)(2,1)S(1)}, bf16[512,512]{1,0:T(8,128)(2,1)}, u32[]{:S(2)}) copy-start(bf16[512,512]{1,0:T(8,128)(2,1)} %constant.5.clone.second_hbm) | copy-start | bytes 1572868
  4.6 1.0 %copy-start.4 = (bf16[512,512]{1,0:T(8,128)(2,1)S(1)}, bf16[512,512]{1,0:T(8,128)(2,1)}, u32[]{:S(2)}) copy-start(bf16[512,512]{1,0:T(8,128)(2,1)} %constant.4.clone.first_hbm) | copy-start | bytes 1572868
  5.6 0.7 %copy-start.5 = (s32[2,2,2]{2,1,0:T(2,128)S(1)}, s32[2,2,2]{2,1,0:T(2,128)}, u32[]{:S(2)}) copy-start(s32[2,2,2]{2,1,0:T(2,128)} %offsets_hbm.1) | copy-start | bytes 100
  6.3 0.7 %copy-start.6 = (s32[2,2]{1,0:T(2,128)S(1)}, s32[2,2]{1,0:T(2,128)}, u32[]{:S(2)}) copy-start(s32[2,2]{1,0:T(2,128)} %positions_hbm.1) | copy-start | bytes 52

commit v3 on v2

--- a/solution.py
+++ b/solution.py
@@ -14,6 +14,7 @@
 RIDGE = 0.05
 FLOOR = 0.25
 MESH = pl.DeviceIdType.MESH
+FLIGHT = 3
 
 
 def inverse_tables(length):
@@ -217,25 +218,36 @@
         peaks[0, t] = jnp.broadcast_to(peak, (8, 128))
 
 
-    for t in range(tl):
-        work(t)
-        if t == 0:
-            pl.semaphore_wait(barrier, n - 1 + m - 1)
-
-        @pl.when(z == 0)
-        def _():
-            for q in range(n - 1, 0, -1):
-                for c in range(2):
-                    right_copy(t, c, q).start()
-
-        @pl.when(z == n - 1)
-        def _():
-            for q in range(n - 1):
-                for c in range(2):
-                    left_copy(t, c, q).start()
-
-    for d in range(1, n):
-        peak_copy(d).start()
+    def mixed_rows():
+        for d in range(1, m):
+            place_copy(d).wait_recv()
+        place_rows = [
+            (places[d, 2 * t : 2 * t + 1, :], places[d, 2 * t + 1 : 2 * t + 2, :])
+            for d in range(m)
+            for t in range(tl)
+        ]
+        return mixing_matrix(place_rows, tiles)
+
+    per_tile = 2 * (n - 1)
+
+    def end_copy(k, side):
+        t, rest = divmod(k, per_tile)
+        d, c = n - 1 - rest // 2, rest % 2
+        return right_copy(t, c, d) if side == 0 else left_copy(t, c, n - 1 - d)
+
+    def push(k):
+        for side, end in ((0, 0), (1, n - 1)):
+            @pl.when(z == end)
+            def _():
+                if k >= FLIGHT:
+                    end_copy(k - FLIGHT, side).wait_send()
+                end_copy(k, side).start()
+
+    early = min(FLIGHT, per_tile)
+    work(0)
+    pl.semaphore_wait(barrier, n - 1 + m - 1)
+    for k in range(early):
+        push(k)
     loads["positions"].wait()
     place = jnp.zeros((8, 128), jnp.float32)
     for t in range(tl):
@@ -246,21 +258,14 @@
 
     for d in range(1, m):
         place_copy(d).start()
-    for d in range(1, m):
-        place_copy(d).wait_recv()
-    place_rows = [None] * tiles
-    for d in range(m):
-        for t in range(tl):
-            place_rows[d * tl + t] = (places[d, 2 * t : 2 * t + 1, :], places[d, 2 * t + 1 : 2 * t + 2, :])
-    mix = mixing_matrix(place_rows, tiles)
+    for t in range(1, tl):
+        work(t)
     for d in range(1, n):
-        peak_copy(d).wait_recv()
+        peak_copy(d).start()
 
     for t in range(tl):
-        peak = peaks[0, t]
-        for d in range(1, n):
-            peak = peak + peaks[d, t]
-        mean_peak = jnp.broadcast_to((peak / led_total)[:1, :1], (rows, length))
+        for k in range(early if t == 0 else t * per_tile, (t + 1) * per_tile):
+            push(k)
         for d in range(n - 1, 0, -1):
             for c in range(2):
                 @pl.when(jnp.logical_and(z > 0, z + d < n))
@@ -276,6 +281,13 @@
                     left_copy(t, c, q).wait_recv()
                     grad[t, c, strip(q)] += from_right[t, c, q]
                     left_copy(t, c, q).start()
+        if t == 0:
+            for d in range(1, n):
+                peak_copy(d).wait_recv()
+        peak = peaks[0, t]
+        for d in range(1, n):
+            peak = peak + peaks[d, t]
+        mean_peak = jnp.broadcast_to((peak / led_total)[:1, :1], (rows, length))
         for c in range(2):
             @pl.when(z > 0)
             def _():
@@ -290,6 +302,8 @@
             gathered[me, t, c] = pupils_ref[t, c, strip(z)] + grad[t, c, strip(z)] / mean_peak
             for d in range(1, m):
                 tile_copy(t, c, d).start()
+        if t == 0:
+            mix = mixed_rows()
 
     for t in range(tl):
         for c in range(2):
@@ -316,13 +330,18 @@
             for d in range(1, m):
                 tile_copy(t, c, d).wait_send()
             for d in range(1, n):
-                @pl.when(z + d < n)
+                @pl.when(jnp.logical_and(z > 0, z + d < n))
                 def _():
                     right_copy(t, c, z + d).wait_send()
 
-                @pl.when(z - d >= 0)
+                @pl.when(jnp.logical_and(z < n - 1, z - d >= 0))
                 def _():
                     left_copy(t, c, z - d).wait_send()
+    for k in range(max(tl * per_tile - FLIGHT, 0), tl * per_tile):
+        for side, end in ((0, 0), (1, n - 1)):
+            @pl.when(z == end)
+            def _():
+                end_copy(k, side).wait_send()
 
 
 def per_device(n, m, spectra, pupils, amplitudes, offsets, positions):
@@ -359,7 +378,7 @@
             dma((tl, 2, m)), dma((tl, 2, m)),
         ],
         compiler_params=pltpu.CompilerParams(
-            collective_id=0, has_side_effects=True, vmem_limit_bytes=40 << 20
+            collective_id=0, has_side_effects=True, vmem_limit_bytes=60 << 20
         ),
     )(*operands)
 

time: 56.4 us -> 41.3 us (0.73); the launches traced: 55.4 us -> 41.1 us
  Pallas kernels: 47.7 us -> 39.5 us
  local copies, waits for them, and re-layouts: 7.68 us -> 1.67 us
    pallas_call x1, Pallas kernels: 47.7 us -> 39.5 us  [per_device(): pl.pallas_call(functools.partial(kernel, n, m, leds * n), out_shape=jax.S...]
    unnamed x15 -> x1, local copies, waits for them, and re-layouts: 7.68 us -> 1.67 us
where the time goes in v3:
time: 41.3 us; the launch traced here: 41.1 us
  Pallas kernels  39.5 us (96%)
  local copies, waits for them, and re-layouts  1.67 us (4%)
    pallas_call x1, Pallas kernels, per_device(): pl.pallas_call(functools.partial(kernel, n, m, leds * n), out_shape=jax.S...  39.5 us
    unnamed x1, local copies, waits for them, and re-layouts  1.67 us

profile of v3, /device:TPU:0, one launch (start us, length us, event | category | flops | bytes accessed | tf_op | source)
XLA Modules:
  0.0 41.1 jit_solution(4166276331108130604)
XLA Ops:
  0.0 39.5 %shard_map.73 = f32[2,2,64,256]{3,2,1,0:T(8,128)} custom-call(bf16[2,2,384,384]{3,2,1,0:T(8,128)(2,1)} %spectra_hbm.1, f32[2,2,256,256]{3,2,1,0:T(8,128)} %pupils_hbm.1, bf16[2,2,256,256]{3,2,1,0:T(8,128)(2,1)} %amps_hbm.1, s32[2,2,2]{2,1,0:T(2,128)} %offsets_hbm.1, s32[2,2]{1,0:T(2,128)} %positions_hbm.1, bf16[512,512]{1,0:T(8,128)(2,1)} %constant.4.clone.first_hbm, ...), custom_call_target="tpu_custom_call" | custom-call | tf_op jit(solution)/shard_map/pallas_call | solution.py:357
  39.5 1.7 %copy.9 = f32[2,2,64,256]{3,2,1,0:T(8,128)} copy(f32[2,2,64,256]{3,2,1,0:T(8,128)} %shard_map.73) | data formatting | bytes 524288

commit v4 on v3

--- a/solution.py
+++ b/solution.py
@@ -14,7 +14,9 @@
 RIDGE = 0.05
 FLOOR = 0.25
 MESH = pl.DeviceIdType.MESH
-FLIGHT = 3
+FLIGHT = 4
+EARLY = 4
+AHEAD = 3
 
 
 def inverse_tables(length):
@@ -105,8 +107,13 @@
     def led_peer(d):
         return {"led": lax.rem(z + d, n)}
 
-    def tile_peer(d):
-        return {"tile": lax.rem(me + d, m)}
+    other = me + 1 - 2 * lax.rem(me, 2)
+
+    def tile_peer(j):
+        return {"tile": lax.rem((other if j % 2 else me) + j // 2 * 2, m)}
+
+    def tile_source(j):
+        return lax.rem((other if j % 2 else me) + m - j // 2 * 2, m)
 
     def strip(q):
         return pl.ds(pl.multiple_of(q * rows, rows), rows)
@@ -157,18 +164,38 @@
             left_send.at[t, c, q], left_recv.at[t, c, q],
             device_id=led_peer(n - 1), device_id_type=MESH)
 
-    def tile_copy(t, c, d):
-        return pltpu.make_async_remote_copy(
-            gathered.at[me, t, c], gathered.at[me, t, c],
-            tile_send.at[t, c, d], tile_recv.at[t, c, d],
-            device_id=tile_peer(d), device_id_type=MESH)
-
-    def tile_arrival(t, c, d):
-        source = lax.rem(me + m - d, m)
-        return pltpu.make_async_remote_copy(
-            gathered.at[me, t, c], gathered.at[source, t, c],
-            tile_send.at[t, c, d], tile_recv.at[t, c, d],
-            device_id=tile_peer(d), device_id_type=MESH)
+    def tile_copy(t, c, j):
+        strip_at = gathered.at[tile_source(j - 1) if j % 2 else me, t, c]
+        return pltpu.make_async_remote_copy(
+            strip_at, strip_at, tile_send.at[t, c, j], tile_recv.at[t, c, j],
+            device_id=tile_peer(1 if j % 2 else j), device_id_type=MESH)
+
+    def tile_arrival(t, c, j):
+        strip_at = gathered.at[tile_source(j), t, c]
+        return pltpu.make_async_remote_copy(
+            strip_at, strip_at, tile_send.at[t, c, j], tile_recv.at[t, c, j],
+            device_id=tile_peer(j), device_id_type=MESH)
+
+    def hand_over(t, c):
+        for j in range(2, m, 2):
+            tile_arrival(t, c, j).wait_recv()
+            tile_copy(t, c, j + 1).start()
+
+    def mix_in(t, c):
+        totals = [jnp.zeros((rows, length), jnp.float32) for _ in range(tl)]
+        for j in range(m):
+            if j % 2:
+                tile_arrival(t, c, j).wait_recv()
+            piece = gathered[tile_source(j), t, c]
+            at = j * tl + t
+            for own in range(tl):
+                share = jnp.broadcast_to(mix[own : own + 1, at : at + 1], (rows, length))
+                totals[own] += share * piece
+        for own in range(tl):
+            if t == 0:
+                out_ref[own, c] = totals[own]
+            else:
+                out_ref[own, c] += totals[own]
 
     def work(t):
         loads["spectra", t].wait()
@@ -243,10 +270,9 @@
                     end_copy(k - FLIGHT, side).wait_send()
                 end_copy(k, side).start()
 
-    early = min(FLIGHT, per_tile)
     work(0)
     pl.semaphore_wait(barrier, n - 1 + m - 1)
-    for k in range(early):
+    for k in range(min(EARLY, per_tile)):
         push(k)
     loads["positions"].wait()
     place = jnp.zeros((8, 128), jnp.float32)
@@ -262,10 +288,11 @@
         work(t)
     for d in range(1, n):
         peak_copy(d).start()
+    later = min(tl * per_tile, per_tile + AHEAD)
+    for k in range(min(EARLY, per_tile), later):
+        push(k)
 
     for t in range(tl):
-        for k in range(early if t == 0 else t * per_tile, (t + 1) * per_tile):
-            push(k)
         for d in range(n - 1, 0, -1):
             for c in range(2):
                 @pl.when(jnp.logical_and(z > 0, z + d < n))
@@ -284,6 +311,9 @@
         if t == 0:
             for d in range(1, n):
                 peak_copy(d).wait_recv()
+        else:
+            for c in range(2):
+                hand_over(t - 1, c)
         peak = peaks[0, t]
         for d in range(1, n):
             peak = peak + peaks[d, t]
@@ -300,26 +330,20 @@
                 grad[t, c, strip(z)] += from_right[t, c, z]
 
             gathered[me, t, c] = pupils_ref[t, c, strip(z)] + grad[t, c, strip(z)] / mean_peak
-            for d in range(1, m):
-                tile_copy(t, c, d).start()
+            for j in (1, *range(2, m, 2)):
+                tile_copy(t, c, j).start()
         if t == 0:
             mix = mixed_rows()
-
-    for t in range(tl):
+            for k in range(later, tl * per_tile):
+                push(k)
+
+    for t in range(tl - 1):
         for c in range(2):
-            totals = [jnp.zeros((rows, length), jnp.float32) for _ in range(tl)]
-            for d in range(m):
-                if d:
-                    tile_arrival(t, c, d).wait_recv()
-                piece = gathered[lax.rem(me + m - d, m), t, c]
-                at = d * tl + t
-                for own in range(tl):
-                    totals[own] += jnp.broadcast_to(mix[own : own + 1, at : at + 1], (rows, length)) * piece
-            for own in range(tl):
-                if t == 0:
-                    out_ref[own, c] = totals[own]
-                else:
-                    out_ref[own, c] += totals[own]
+            mix_in(t, c)
+    for c in range(2):
+        hand_over(tl - 1, c)
+    for c in range(2):
+        mix_in(tl - 1, c)
 
     for d in range(1, m):
         place_copy(d).wait_send()

time: 41.3 us -> 37.8 us (0.915)
  Pallas kernels: 39.5 us -> 36 us
    pallas_call x1, Pallas kernels: 39.5 us -> 36 us  [per_device(): pl.pallas_call(functools.partial(kernel, n, m, leds * n), out_shape=jax.S...]
where the time goes in v4:
time: 37.8 us; the launch traced here: 37.6 us
  Pallas kernels  36 us (95%)
  local copies, waits for them, and re-layouts  1.67 us (4%)
    pallas_call x1, Pallas kernels, per_device(): pl.pallas_call(functools.partial(kernel, n, m, leds * n), out_shape=jax.S...  36 us
    unnamed x1, local copies, waits for them, and re-layouts  1.67 us

profile of v4, /device:TPU:0, one launch (start us, length us, event | category | flops | bytes accessed | tf_op | source)
XLA Modules:
  0.0 37.6 jit_solution(2075767242978465478)
XLA Ops:
  0.0 36.0 %shard_map.73 = f32[2,2,64,256]{3,2,1,0:T(8,128)} custom-call(bf16[2,2,384,384]{3,2,1,0:T(8,128)(2,1)} %spectra_hbm.1, f32[2,2,256,256]{3,2,1,0:T(8,128)} %pupils_hbm.1, bf16[2,2,256,256]{3,2,1,0:T(8,128)(2,1)} %amps_hbm.1, s32[2,2,2]{2,1,0:T(2,128)} %offsets_hbm.1, s32[2,2]{1,0:T(2,128)} %positions_hbm.1, bf16[512,512]{1,0:T(8,128)(2,1)} %constant.4.clone.first_hbm, ...), custom_call_target="tpu_custom_call" | custom-call | tf_op jit(solution)/shard_map/pallas_call | solution.py:381
  36.0 1.7 %copy.9 = f32[2,2,64,256]{3,2,1,0:T(8,128)} copy(f32[2,2,64,256]{3,2,1,0:T(8,128)} %shard_map.73) | data formatting | bytes 524288
